TPU v7x, 256 devices: a whole 4x4x8 slice. The times are simulated.
256 devices in a mesh: wide: 32 (over z_lo, y, core), narrow: 8 (over z_hi, x).
Axes of the slice: x: 4, y: 4, z: 8 (z_hi: 2, z_lo: 4; z = z_hi * 4 + z_lo), core: 2. Of those that a mesh axis runs over, the one named last changes fastest.
Arguments:
- pressure: float32 [512, 512, 1024], P(('narrow', 'wide')), may hold values from -6 to 6
- relax_freq: float32 [2], replicated, may hold values from 4 to 64
- relax_depth: float32 [2], replicated, may hold values from 0.1 to 0.6
Outputs:
- advanced: float32 [512, 512, 1024], P(('narrow', 'wide'))
All inputs are finite; a program needn't handle non-finite values.
Results may differ from a plain program's by a relative error of at most 0.000084.
Values sent between devices are 32-bit elements; how exact they have to be, the bound alone decides.
A program may use at most 128 MiB of HBM per device.

v0:
```python
import functools

import jax
import jax.numpy as jnp
import ml_dtypes
import numpy as np
from jax import lax
from jax.experimental import pallas as pl
from jax.experimental.pallas import tpu as pltpu
from jax.sharding import PartitionSpec as P

SUBSTEPS = 3
STEPS = 2 * SUBSTEPS
WAVE_BREAKING = 0.1
RATE_TOP = 0.2

NY = 512
NT = 1024
HALF = NT // 2
LANES = 128
CHUNKS = (NT // 2) // LANES
PAD = 8
BLOCK = 256
ROWS = 2
MESH = pl.DeviceIdType.MESH


def chunk_bins(chunk):
    return 2 * (np.arange(LANES) + LANES * (chunk % 2)) + chunk // 2


def split_table(table):
    high = table.astype(ml_dtypes.bfloat16)
    low = (table - high.astype(np.float64)).astype(ml_dtypes.bfloat16)
    return high, low


def forward_tables():
    time = np.arange(HALF)
    tables = []
    for chunk in range(CHUNKS):
        angle = 2.0 * np.pi * (time[:, None] * chunk_bins(chunk)[None, :] % NT) / NT
        tables.append(split_table(np.concatenate([np.cos(angle), -np.sin(angle)], axis=1)))
    return np.stack([np.stack(pair) for pair in tables])


def inverse_tables():
    time = np.arange(HALF)
    tables = []
    for chunk in range(CHUNKS):
        bins = chunk_bins(chunk)
        angle = 2.0 * np.pi * (bins[:, None] * time[None, :] % NT) / NT
        weight = (np.where(bins == 0, 1.0, 2.0) / NT)[:, None]
        parts = []
        for table in (np.cos(angle) * weight, -np.sin(angle) * weight):
            high, low = split_table(table)
            parts.append(np.concatenate([high, high, low], axis=0))
        tables.append(np.stack(parts))
    return np.stack(tables)


def split_values(values):
    high = values.astype(jnp.bfloat16)
    low = (values - high.astype(jnp.float32)).astype(jnp.bfloat16)
    return high, low


def dot(lhs, rhs):
    return jnp.dot(lhs, rhs, preferred_element_type=jnp.float32)


def step_kernel(
    narrow_size, wide_size,
    freq_ref, depth_ref, pressure_ref, forward_ref, inverse_ref,
    out_ref,
    waves, fields, landed, fwd, inv, sums, factors,
    wave_sems, table_sems, out_sems, send_sems, recv_sems,
):
    count = narrow_size * wide_size
    me = lax.axis_index("narrow") * wide_size + lax.axis_index("wide")
    core = lax.rem(me, 2)

    def device(index):
        return {"narrow": index // wide_size, "wide": lax.rem(index, wide_size)}

    def partner(direction):
        return me - 1 + 2 * direction

    def has_partner(direction):
        other = partner(direction)
        return jnp.logical_and(other >= 0, other < count)

    def row_at(turn):
        return lax.rem(core + turn, 2)

    blocks = NY // BLOCK

    def wave_copy(row, block):
        rows = pl.ds(pl.multiple_of(block * BLOCK, BLOCK), BLOCK)
        return pltpu.make_async_copy(
            pressure_ref.at[row, rows], waves.at[row, rows], wave_sems.at[row, block]
        )

    def table_copy(chunk):
        return pltpu.make_async_copy(forward_ref.at[chunk], fwd.at[chunk], table_sems.at[chunk])

    inverse_copy = pltpu.make_async_copy(inverse_ref, inv, table_sems.at[CHUNKS])

    wave_copy(row_at(0), 0).start()
    table_copy(0).start()
    for block in range(1, blocks):
        wave_copy(row_at(0), block).start()
    for chunk in range(1, CHUNKS):
        table_copy(chunk).start()
    for block in range(blocks):
        wave_copy(row_at(1), block).start()
    inverse_copy.start()

    barrier = pltpu.get_barrier_semaphore()
    for direction in range(2):
        @pl.when(has_partner(direction))
        def _():
            pl.semaphore_signal(
                barrier, inc=1, device_id=device(partner(direction)), device_id_type=MESH
            )

    lane = lax.broadcasted_iota(jnp.int32, (8, LANES), 1)
    for chunk in range(CHUNKS):
        bins = (2 * (lane + LANES * (chunk % 2)) + chunk // 2).astype(jnp.float32)
        total_re = jnp.zeros_like(bins)
        total_im = jnp.zeros_like(bins)
        for process in range(2):
            ratio = bins / freq_ref[process]
            scaled = depth_ref[process] / (1.0 + ratio * ratio)
            total_re = total_re + scaled * ratio * ratio
            total_im = total_im + scaled * ratio
        amplitude = jnp.exp(-total_re)
        factors[0, chunk] = amplitude * jnp.cos(total_im)
        factors[1, chunk] = -amplitude * jnp.sin(total_im)
        factors[2, chunk] = (
            RATE_TOP
            * jnp.minimum(bins, 1.0)
            * jnp.minimum(1.0, float(NT // 4) / jnp.maximum(bins, 1.0))
        )

    zero_rows = jnp.zeros((PAD, LANES), jnp.float32)
    for part in range(2):
        for chunk in range(CHUNKS):
            for row in range(ROWS):
                fields[part, chunk, row, 0:PAD] = zero_rows
                fields[part, chunk, row, PAD + NY:] = zero_rows

    pl.semaphore_wait(
        barrier, has_partner(0).astype(jnp.int32) + has_partner(1).astype(jnp.int32)
    )

    def slot(message, direction):
        return 2 * message + direction

    def send(message, part, chunk, direction, start=0, size=NY):
        return pltpu.make_async_remote_copy(
            src_ref=fields.at[part, chunk, direction, pl.ds(PAD + start, size)],
            dst_ref=landed.at[slot(message, direction), pl.ds(start, size)],
            send_sem=send_sems.at[message, direction],
            recv_sem=recv_sems.at[message, direction],
            device_id=device(partner(direction)),
            device_id_type=MESH,
        )

    def forward_block(row, block):
        rows = pl.ds(pl.multiple_of(block * BLOCK, BLOCK), BLOCK)
        inner = pl.ds(pl.multiple_of(PAD + block * BLOCK, PAD), BLOCK)
        wave_copy(row, block).wait()
        wave = waves[row, rows]
        squared = wave * wave
        time = lax.broadcasted_iota(jnp.int32, (BLOCK, NT), 1)
        after = jnp.where(time == NT - 1, 0.0, pltpu.roll(squared, NT - 1, 1))
        before = jnp.where(time == 0, 0.0, pltpu.roll(squared, 1, 1))
        steep = wave + WAVE_BREAKING * 0.25 * (after - before)
        first, second = steep[:, :HALF], steep[:, HALF:]
        pairs = (split_values(first + second), split_values(first - second))
        for chunk in range(CHUNKS):
            high, low = pairs[chunk // 2]
            both = (
                dot(high, fwd[chunk, 0]) + dot(low, fwd[chunk, 0]) + dot(high, fwd[chunk, 1])
            )
            re, im = both[:, :LANES], both[:, LANES:]
            factor_re = factors[0, chunk, 0:1]
            factor_im = factors[1, chunk, 0:1]
            fields[0, chunk, row, inner] = re * factor_re - im * factor_im
            fields[1, chunk, row, inner] = re * factor_im + im * factor_re

    for chunk in range(CHUNKS):
        table_copy(chunk).wait()

    def forward_row(turn, carry):
        row = row_at(turn)

        def one(block, inner_carry):
            forward_block(row, block)

            return inner_carry

        lax.fori_loop(0, blocks, one, 0)

        @pl.when(has_partner(row))
        def _():
            for chunk in range(CHUNKS):
                send(chunk, 1, chunk, row).start()

        return carry

    lax.fori_loop(0, 2, forward_row, 0)

    @pl.when(jnp.logical_or(me == 0, me == count - 1))
    def _():
        landed[2 * STEPS * CHUNKS] = jnp.zeros((NY, LANES), jnp.float32)

    sums[...] = jnp.zeros_like(sums)

    def half_step(message, part, chunk, row):
        halo_from = 1 - row
        at = jnp.where(has_partner(row), slot(message, halo_from), 2 * STEPS * CHUNKS)
        other = 1 - part
        sign = (2 * part - 1).astype(jnp.float32)
        rate = factors[2, chunk, 0:1] * sign
        size = 64
        for start in range(0, NY, size):
            base = PAD + start
            center = fields[other, chunk, row, base:base + size]
            below = fields[other, chunk, row, base - 1:base - 1 + size]
            above = fields[other, chunk, row, base + 1:base + 1 + size]
            beside = fields[other, chunk, 1 - row, base:base + size]
            halo = landed[at, start:start + size]
            laplacian = (halo + beside) + (below + above) - 4.0 * center
            fields[part, chunk, row, base:base + size] += rate * laplacian

    def wait_for(message, part, chunk):
        for direction in range(2):
            @pl.when(has_partner(1 - direction))
            def _():
                send(message, 1 - part, chunk, direction).wait_recv()

    def wait_sent(message, part, chunk):
        for direction in range(2):
            @pl.when(has_partner(direction))
            def _():
                send(message, 1 - part, chunk, direction).wait_send()

    def advance(message, carry):
        step = message // CHUNKS
        chunk = lax.rem(message, CHUNKS)
        part = lax.rem(step, 2)
        wait_for(message, part, chunk)

        @pl.when(step > 0)
        def _():
            wait_sent(message - CHUNKS, 1 - part, chunk)

        for turn in range(2):
            row = row_at(turn)
            half_step(message, part, chunk, row)

            @pl.when(jnp.logical_and(has_partner(row), step < STEPS - 1))
            def _():
                send(message + CHUNKS, part, chunk, row).start()

        @pl.when(step >= STEPS - 2)
        def _():
            for row in range(ROWS):
                def gather(block, inner_carry):
                    inner = pl.ds(pl.multiple_of(PAD + block * BLOCK, PAD), BLOCK)
                    rows = pl.ds(pl.multiple_of(block * BLOCK, BLOCK), BLOCK)
                    high, low = split_values(fields[part, chunk, row, inner])
                    terms = jnp.concatenate([high, low, high], axis=1)
                    sums[chunk // 2, row, rows] += dot(terms, inv[chunk, part])
                    return inner_carry

                lax.fori_loop(0, blocks, gather, 0)

        return carry

    inverse_copy.wait()
    lax.fori_loop(0, STEPS * CHUNKS, advance, 0)

    def out_copy(row, block, side):
        rows = pl.ds(pl.multiple_of(block * BLOCK, BLOCK), BLOCK)
        return pltpu.make_async_copy(
            sums.at[side, row, rows],
            out_ref.at[row, rows, pl.ds(side * HALF, HALF)],
            out_sems.at[row, block, side],
        )

    for row in range(ROWS):
        for block in range(blocks):
            rows = slice(block * BLOCK, (block + 1) * BLOCK)
            even, odd = sums[0, row, rows], sums[1, row, rows]
            sums[0, row, rows] = even + odd
            sums[1, row, rows] = even - odd
            for side in range(2):
                out_copy(row, block, side).start()
    for row in range(ROWS):
        for block in range(blocks):
            for side in range(2):
                out_copy(row, block, side).wait()
    for chunk in range(CHUNKS):
        wait_sent((STEPS - 1) * CHUNKS + chunk, 1, chunk)


def shards(narrow_size, wide_size, pressure, relax_freq, relax_depth):
    blocks = NY // BLOCK
    messages = STEPS * CHUNKS
    hbm = pl.BlockSpec(memory_space=pltpu.HBM)
    smem = pl.BlockSpec(memory_space=pltpu.SMEM)
    f32, bf16 = jnp.float32, jnp.bfloat16
    dma = pltpu.SemaphoreType.DMA
    return pl.pallas_call(
        functools.partial(step_kernel, narrow_size, wide_size),
        out_shape=jax.ShapeDtypeStruct((ROWS, NY, NT), f32),
        in_specs=[smem, smem, hbm, hbm, hbm],
        out_specs=hbm,
        scratch_shapes=[
            pltpu.VMEM((ROWS, NY, NT), f32),
            pltpu.VMEM((2, CHUNKS, ROWS, NY + 2 * PAD, LANES), f32),
            pltpu.VMEM((2 * messages + 1, NY, LANES), f32),
            pltpu.VMEM((CHUNKS, 2, HALF, 2 * LANES), bf16),
            pltpu.VMEM((CHUNKS, 2, 3 * LANES, HALF), bf16),
            pltpu.VMEM((2, ROWS, NY, HALF), f32),
            pltpu.VMEM((3, CHUNKS, 8, LANES), f32),
            dma((ROWS, blocks)),
            dma((CHUNKS + 1,)),
            dma((ROWS, blocks, 2)),
            dma((messages, 2)),
            dma((messages, 2)),
        ],
        compiler_params=pltpu.CompilerParams(
            collective_id=0, has_side_effects=True, vmem_limit_bytes=56 * 2**20
        ),
        cost_estimate=pl.CostEstimate(
            flops=2 * 2 * 3 * ROWS * NY * HALF * NT, bytes_accessed=14 * 2**20, transcendentals=0
        ),
    )(relax_freq, relax_depth, pressure, jnp.asarray(forward_tables()), jnp.asarray(inverse_tables()))


def solution(mesh):
    placed = (P(("narrow", "wide"), None, None), P(), P())
    return jax.shard_map(
        functools.partial(shards, mesh.shape["narrow"], mesh.shape["wide"]),
        mesh=mesh,
        in_specs=placed,
        out_specs=P(("narrow", "wide"), None, None),
        check_vma=False,
    )
```

profile of v0, /device:TPU:6, one launch (start us, length us, event | category | flops | bytes accessed | tf_op | source)
XLA Modules:
  0.0 90.4 jit_solution(17057293785923607771)
XLA Ops:
  0.0 85.6 %shard_map.55 = f32[2,512,1024]{2,1,0:T(8,128)} custom-call(f32[2]{0:T(128)} %freq_ref.1, f32[2]{0:T(128)} %depth_ref.1, f32[2,512,1024]{2,1,0:T(8,128)} %pressure_ref.1, bf16[4,2,512,256]{3,2,1,0:T(8,128)(2,1)} %constant.4.clone.forward_ref, bf16[4,2,384,512]{3,2,1,0:T(8,128)(2,1)} %constant.5.clone.inverse_ref), custom_call_target="tpu_custom_call" | custom-call | flops 6442450944 | bytes 14680064 | tf_op jit(solution)/shard_map/pallas_call | solution.py:317
  85.6 4.8 %copy.7 = f32[2,512,1024]{2,1,0:T(8,128)} copy(f32[2,512,1024]{2,1,0:T(8,128)} %shard_map.55) | data formatting | bytes 8388608
where the time goes:
time: 90.5 us; the launch traced here: 90.4 us
  Pallas kernels  85.6 us (95%)
  local copies, waits for them, and re-layouts  4.79 us (5%)
    pallas_call x1, Pallas kernels, shards(): pl.pallas_call(functools.partial(step_kernel, narrow_size, wide_size), ou...  85.6 us
    unnamed x1, local copies, waits for them, and re-layouts  4.79 us

commit v1 on v0

--- a/solution.py
+++ b/solution.py
@@ -20,7 +20,10 @@
 LANES = 128
 CHUNKS = (NT // 2) // LANES
 PAD = 8
-BLOCK = 256
+BLOCK = 128
+GATHER = 256
+PIECES = 4
+EAGER = 2
 ROWS = 2
 MESH = pl.DeviceIdType.MESH
 
@@ -73,8 +76,8 @@
     narrow_size, wide_size,
     freq_ref, depth_ref, pressure_ref, forward_ref, inverse_ref,
     out_ref,
-    waves, fields, landed, fwd, inv, sums, factors,
-    wave_sems, table_sems, out_sems, send_sems, recv_sems,
+    waves, fields, landed, fwd, inv, factors,
+    wave_sems, table_sems, send_sems, recv_sems, last_send_sems, last_recv_sems,
 ):
     count = narrow_size * wide_size
     me = lax.axis_index("narrow") * wide_size + lax.axis_index("wide")
@@ -167,7 +170,7 @@
             device_id_type=MESH,
         )
 
-    def forward_block(row, block):
+    def forward_block(row, block, first):
         rows = pl.ds(pl.multiple_of(block * BLOCK, BLOCK), BLOCK)
         inner = pl.ds(pl.multiple_of(PAD + block * BLOCK, PAD), BLOCK)
         wave_copy(row, block).wait()
@@ -177,9 +180,11 @@
         after = jnp.where(time == NT - 1, 0.0, pltpu.roll(squared, NT - 1, 1))
         before = jnp.where(time == 0, 0.0, pltpu.roll(squared, 1, 1))
         steep = wave + WAVE_BREAKING * 0.25 * (after - before)
-        first, second = steep[:, :HALF], steep[:, HALF:]
-        pairs = (split_values(first + second), split_values(first - second))
+        early, late = steep[:, :HALF], steep[:, HALF:]
+        pairs = (split_values(early + late), split_values(early - late))
         for chunk in range(CHUNKS):
+            if first:
+                table_copy(chunk).wait()
             high, low = pairs[chunk // 2]
             both = (
                 dot(high, fwd[chunk, 0]) + dot(low, fwd[chunk, 0]) + dot(high, fwd[chunk, 1])
@@ -187,45 +192,43 @@
             re, im = both[:, :LANES], both[:, LANES:]
             factor_re = factors[0, chunk, 0:1]
             factor_im = factors[1, chunk, 0:1]
+            fields[1, chunk, row, inner] = re * factor_im + im * factor_re
+            if chunk < EAGER:
+                @pl.when(has_partner(row))
+                def _():
+                    send(chunk, 1, chunk, row, block * BLOCK, BLOCK).start()
             fields[0, chunk, row, inner] = re * factor_re - im * factor_im
-            fields[1, chunk, row, inner] = re * factor_im + im * factor_re
-
-    for chunk in range(CHUNKS):
-        table_copy(chunk).wait()
-
-    def forward_row(turn, carry):
-        row = row_at(turn)
-
-        def one(block, inner_carry):
-            forward_block(row, block)
-
-            return inner_carry
-
-        lax.fori_loop(0, blocks, one, 0)
+
+    def forward_row(row, first):
+        if first:
+            forward_block(row, 0, True)
+
+        def one(block, carry):
+            forward_block(row, block, False)
+            return carry
+
+        lax.fori_loop(1 if first else 0, blocks, one, 0)
 
         @pl.when(has_partner(row))
         def _():
-            for chunk in range(CHUNKS):
+            for chunk in range(EAGER, CHUNKS):
                 send(chunk, 1, chunk, row).start()
 
-        return carry
-
-    lax.fori_loop(0, 2, forward_row, 0)
+    forward_row(row_at(0), True)
+    forward_row(row_at(1), False)
 
     @pl.when(jnp.logical_or(me == 0, me == count - 1))
     def _():
         landed[2 * STEPS * CHUNKS] = jnp.zeros((NY, LANES), jnp.float32)
 
-    sums[...] = jnp.zeros_like(sums)
-
-    def half_step(message, part, chunk, row):
+    def half_step(message, part, chunk, row, first_row=0, count_rows=NY):
         halo_from = 1 - row
         at = jnp.where(has_partner(row), slot(message, halo_from), 2 * STEPS * CHUNKS)
         other = 1 - part
-        sign = (2 * part - 1).astype(jnp.float32)
+        sign = jnp.float32(2 * part - 1)
         rate = factors[2, chunk, 0:1] * sign
         size = 64
-        for start in range(0, NY, size):
+        for start in range(first_row, first_row + count_rows, size):
             base = PAD + start
             center = fields[other, chunk, row, base:base + size]
             below = fields[other, chunk, row, base - 1:base - 1 + size]
@@ -235,76 +238,144 @@
             laplacian = (halo + beside) + (below + above) - 4.0 * center
             fields[part, chunk, row, base:base + size] += rate * laplacian
 
-    def wait_for(message, part, chunk):
-        for direction in range(2):
-            @pl.when(has_partner(1 - direction))
-            def _():
-                send(message, 1 - part, chunk, direction).wait_recv()
-
-    def wait_sent(message, part, chunk):
-        for direction in range(2):
-            @pl.when(has_partner(direction))
-            def _():
-                send(message, 1 - part, chunk, direction).wait_send()
+    def wait_for(message, part, chunk, row):
+        @pl.when(has_partner(row))
+        def _():
+            send(message, 1 - part, chunk, 1 - row).wait_recv()
+
+    def wait_sent(message, part, chunk, direction):
+        @pl.when(has_partner(direction))
+        def _():
+            send(message, 1 - part, chunk, direction).wait_send()
+
+    def terms_of(part, chunk, row, start, size):
+        high, low = split_values(fields[part, chunk, row, pl.ds(PAD + start, size)])
+        return dot(jnp.concatenate([high, low, high], axis=1), inv[chunk, part])
+
+    def gather(part, chunk, fresh):
+        for row in range(ROWS):
+            for start in range(0, NY, GATHER):
+                terms = terms_of(part, chunk, row, start, GATHER)
+                rows = slice(start, start + GATHER)
+                side = slice(0, HALF) if chunk < CHUNKS // 2 else slice(HALF, NT)
+                if fresh:
+                    out_ref[row, rows, side] = terms
+                else:
+                    out_ref[row, rows, side] += terms
 
     def advance(message, carry):
         step = message // CHUNKS
         chunk = lax.rem(message, CHUNKS)
         part = lax.rem(step, 2)
-        wait_for(message, part, chunk)
 
         @pl.when(step > 0)
         def _():
-            wait_sent(message - CHUNKS, 1 - part, chunk)
+            for direction in range(2):
+                wait_sent(message - CHUNKS, 1 - part, chunk, direction)
 
         for turn in range(2):
             row = row_at(turn)
+            wait_for(message, part, chunk, row)
             half_step(message, part, chunk, row)
 
-            @pl.when(jnp.logical_and(has_partner(row), step < STEPS - 1))
+            @pl.when(has_partner(row))
             def _():
                 send(message + CHUNKS, part, chunk, row).start()
 
-        @pl.when(step >= STEPS - 2)
-        def _():
-            for row in range(ROWS):
-                def gather(block, inner_carry):
-                    inner = pl.ds(pl.multiple_of(PAD + block * BLOCK, PAD), BLOCK)
-                    rows = pl.ds(pl.multiple_of(block * BLOCK, BLOCK), BLOCK)
-                    high, low = split_values(fields[part, chunk, row, inner])
-                    terms = jnp.concatenate([high, low, high], axis=1)
-                    sums[chunk // 2, row, rows] += dot(terms, inv[chunk, part])
-                    return inner_carry
-
-                lax.fori_loop(0, blocks, gather, 0)
-
         return carry
 
+    lax.fori_loop(0, (STEPS - 2) * CHUNKS, advance, 0)
     inverse_copy.wait()
-    lax.fori_loop(0, STEPS * CHUNKS, advance, 0)
-
-    def out_copy(row, block, side):
-        rows = pl.ds(pl.multiple_of(block * BLOCK, BLOCK), BLOCK)
-        return pltpu.make_async_copy(
-            sums.at[side, row, rows],
-            out_ref.at[row, rows, pl.ds(side * HALF, HALF)],
-            out_sems.at[row, block, side],
+
+    piece_rows = NY // PIECES
+    last = STEPS * CHUNKS - 1
+
+    def piece_copy(piece, direction):
+        start = piece * piece_rows
+        return pltpu.make_async_remote_copy(
+            src_ref=fields.at[0, CHUNKS - 1, direction, pl.ds(PAD + start, piece_rows)],
+            dst_ref=landed.at[slot(last, direction), pl.ds(start, piece_rows)],
+            send_sem=last_send_sems.at[piece],
+            recv_sem=last_recv_sems.at[piece],
+            device_id=device(partner(direction)),
+            device_id_type=MESH,
         )
 
+    leaving, staying = row_at(0), row_at(1)
+
+    for chunk in range(CHUNKS):
+        message = (STEPS - 2) * CHUNKS + chunk
+        for direction in range(2):
+            wait_sent(message - CHUNKS, 1, chunk, direction)
+        wait_for(message, 0, chunk, leaving)
+        if chunk < CHUNKS - 1:
+            half_step(message, 0, chunk, leaving)
+
+            @pl.when(has_partner(leaving))
+            def _():
+                send(message + CHUNKS, 0, chunk, leaving).start()
+        else:
+            for piece in range(PIECES):
+                half_step(message, 0, chunk, leaving, piece * piece_rows, piece_rows)
+
+                @pl.when(has_partner(leaving))
+                def _():
+                    piece_copy(piece, leaving).start()
+        wait_for(message, 0, chunk, staying)
+        half_step(message, 0, chunk, staying)
+
+        @pl.when(has_partner(staying))
+        def _():
+            send(message + CHUNKS, 0, chunk, staying).start()
+
+        gather(0, chunk, chunk % 2 == 0)
+
+    for chunk in range(CHUNKS - 1):
+        message = (STEPS - 1) * CHUNKS + chunk
+        for direction in range(2):
+            wait_sent(message - CHUNKS, 0, chunk, direction)
+        for row in (staying, leaving):
+            wait_for(message, 1, chunk, row)
+            half_step(message, 1, chunk, row)
+        gather(1, chunk, False)
+
+    def combine(row, rows):
+        even, odd = out_ref[row, rows, :HALF], out_ref[row, rows, HALF:]
+        out_ref[row, rows, :HALF] = even + odd
+        out_ref[row, rows, HALF:] = even - odd
+
     for row in range(ROWS):
-        for block in range(blocks):
-            rows = slice(block * BLOCK, (block + 1) * BLOCK)
-            even, odd = sums[0, row, rows], sums[1, row, rows]
-            sums[0, row, rows] = even + odd
-            sums[1, row, rows] = even - odd
-            for side in range(2):
-                out_copy(row, block, side).start()
-    for row in range(ROWS):
-        for block in range(blocks):
-            for side in range(2):
-                out_copy(row, block, side).wait()
+        for start in range(0, NY, 64):
+            combine(row, slice(start, start + 64))
+
+    def finish(row, start, size):
+        half_step(last, 1, CHUNKS - 1, row, start, size)
+        terms = terms_of(1, CHUNKS - 1, row, start, size)
+        rows = slice(start, start + size)
+        out_ref[row, rows, :HALF] += terms
+        out_ref[row, rows, HALF:] -= terms
+
+    for direction in range(2):
+        wait_sent(last - CHUNKS, 0, CHUNKS - 1, direction)
+    wait_for(last, 1, CHUNKS - 1, staying)
+    for start in range(0, NY, GATHER):
+        finish(staying, start, GATHER)
+    for piece in range(PIECES):
+        @pl.when(has_partner(leaving))
+        def _():
+            piece_copy(piece, 1 - leaving).wait_recv()
+
+        finish(leaving, piece * piece_rows, piece_rows)
+
     for chunk in range(CHUNKS):
-        wait_sent((STEPS - 1) * CHUNKS + chunk, 1, chunk)
+        message = (STEPS - 1) * CHUNKS + chunk
+        wait_sent(message, 1, chunk, staying)
+        if chunk < CHUNKS - 1:
+            wait_sent(message, 1, chunk, leaving)
+    for piece in range(PIECES):
+        @pl.when(has_partner(leaving))
+        def _():
+            piece_copy(piece, leaving).wait_send()
 
 
 def shards(narrow_size, wide_size, pressure, relax_freq, relax_depth):
@@ -316,25 +387,25 @@
     dma = pltpu.SemaphoreType.DMA
     return pl.pallas_call(
         functools.partial(step_kernel, narrow_size, wide_size),
-        out_shape=jax.ShapeDtypeStruct((ROWS, NY, NT), f32),
+        out_shape=pltpu.VMEM((ROWS, NY, NT), f32),
         in_specs=[smem, smem, hbm, hbm, hbm],
-        out_specs=hbm,
+        out_specs=pl.BlockSpec(memory_space=pltpu.VMEM),
         scratch_shapes=[
             pltpu.VMEM((ROWS, NY, NT), f32),
             pltpu.VMEM((2, CHUNKS, ROWS, NY + 2 * PAD, LANES), f32),
             pltpu.VMEM((2 * messages + 1, NY, LANES), f32),
             pltpu.VMEM((CHUNKS, 2, HALF, 2 * LANES), bf16),
             pltpu.VMEM((CHUNKS, 2, 3 * LANES, HALF), bf16),
-            pltpu.VMEM((2, ROWS, NY, HALF), f32),
             pltpu.VMEM((3, CHUNKS, 8, LANES), f32),
             dma((ROWS, blocks)),
             dma((CHUNKS + 1,)),
-            dma((ROWS, blocks, 2)),
             dma((messages, 2)),
             dma((messages, 2)),
+            dma((PIECES,)),
+            dma((PIECES,)),
         ],
         compiler_params=pltpu.CompilerParams(
-            collective_id=0, has_side_effects=True, vmem_limit_bytes=56 * 2**20
+            collective_id=0, has_side_effects=True, vmem_limit_bytes=59 * 2**20
         ),
         cost_estimate=pl.CostEstimate(
             flops=2 * 2 * 3 * ROWS * NY * HALF * NT, bytes_accessed=14 * 2**20, transcendentals=0

time: 90.5 us -> 82.2 us (0.908)
  Pallas kernels: 85.6 us -> 80.1 us
  local copies, waits for them, and re-layouts: 4.79 us -> 2.02 us
    pallas_call x1, Pallas kernels: 85.6 us -> 80.1 us  [shards(): pl.pallas_call(functools.partial(step_kernel, narrow_size, wide_size), ou...]
    unnamed x1, local copies, waits for them, and re-layouts: 4.79 us -> 2.02 us
where the time goes in v1:
time: 82.2 us; the launch traced here: 82.1 us
  Pallas kernels  80.1 us (97%)
  local copies, waits for them, and re-layouts  2.02 us (2%)
    pallas_call x1, Pallas kernels, shards(): pl.pallas_call(functools.partial(step_kernel, narrow_size, wide_size), ou...  80.1 us
    unnamed x1, local copies, waits for them, and re-layouts  2.02 us

profile of v1, /device:TPU:6, one launch (start us, length us, event | category | flops | bytes accessed | tf_op | source)
XLA Modules:
  0.0 82.1 jit_solution(1537320446938522788)
XLA Ops:
  0.0 80.1 %shard_map.55 = f32[2,512,1024]{2,1,0:T(8,128)S(1)} custom-call(f32[2]{0:T(128)} %freq_ref.1, f32[2]{0:T(128)} %depth_ref.1, f32[2,512,1024]{2,1,0:T(8,128)} %pressure_ref.1, bf16[4,2,512,256]{3,2,1,0:T(8,128)(2,1)} %constant.4.clone.forward_ref, bf16[4,2,384,512]{3,2,1,0:T(8,128)(2,1)} %constant.5.clone.inverse_ref), custom_call_target="tpu_custom_call" | custom-call | flops 6442450944 | bytes 14680064 | tf_op jit(solution)/shard_map/pallas_call | solution.py:388
  80.1 2.0 %copy.7 = f32[2,512,1024]{2,1,0:T(8,128)} copy(f32[2,512,1024]{2,1,0:T(8,128)S(1)} %shard_map.55) | data formatting | bytes 8388608

commit v2 on v1

--- a/solution.py
+++ b/solution.py
@@ -20,12 +20,18 @@
 LANES = 128
 CHUNKS = (NT // 2) // LANES
 PAD = 8
-BLOCK = 128
+LEADING = (96, 416)
+TRAILING = (256, 256)
 GATHER = 256
-PIECES = 4
-EAGER = 2
+PIECES = (384, 128)
+EAGER = 4
+SLOTS = 2 * CHUNKS
 ROWS = 2
 MESH = pl.DeviceIdType.MESH
+
+
+def starts(sizes):
+    return [sum(sizes[:index]) for index in range(len(sizes))]
 
 
 def chunk_bins(chunk):
@@ -76,8 +82,8 @@
     narrow_size, wide_size,
     freq_ref, depth_ref, pressure_ref, forward_ref, inverse_ref,
     out_ref,
-    waves, fields, landed, fwd, inv, factors,
-    wave_sems, table_sems, send_sems, recv_sems, last_send_sems, last_recv_sems,
+    waves, fields, landed, fwd, inv, factors, freqs, depths,
+    wave_sems, table_sems, scalar_sems, send_sems, recv_sems, last_send_sems, last_recv_sems,
 ):
     count = narrow_size * wide_size
     me = lax.axis_index("narrow") * wide_size + lax.axis_index("wide")
@@ -96,29 +102,34 @@
     def row_at(turn):
         return lax.rem(core + turn, 2)
 
-    blocks = NY // BLOCK
-
-    def wave_copy(row, block):
-        rows = pl.ds(pl.multiple_of(block * BLOCK, BLOCK), BLOCK)
+    def wave_copy(turn, block):
+        sizes = (LEADING, TRAILING)[turn]
+        rows = pl.ds(starts(sizes)[block], sizes[block])
         return pltpu.make_async_copy(
-            pressure_ref.at[row, rows], waves.at[row, rows], wave_sems.at[row, block]
+            pressure_ref.at[row_at(turn), rows],
+            waves.at[row_at(turn), rows],
+            wave_sems.at[turn * len(LEADING) + block],
         )
 
     def table_copy(chunk):
         return pltpu.make_async_copy(forward_ref.at[chunk], fwd.at[chunk], table_sems.at[chunk])
 
     inverse_copy = pltpu.make_async_copy(inverse_ref, inv, table_sems.at[CHUNKS])
-
-    wave_copy(row_at(0), 0).start()
+    freq_copy = pltpu.make_async_copy(freq_ref, freqs, scalar_sems.at[0])
+    depth_copy = pltpu.make_async_copy(depth_ref, depths, scalar_sems.at[1])
+
+    freq_copy.start()
+    depth_copy.start()
+    wave_copy(0, 0).start()
     table_copy(0).start()
-    for block in range(1, blocks):
-        wave_copy(row_at(0), block).start()
-    for chunk in range(1, CHUNKS):
+    wave_copy(0, 1).start()
+    table_copy(1).start()
+    for block in range(2, len(LEADING)):
+        wave_copy(0, block).start()
+    for chunk in range(2, CHUNKS):
         table_copy(chunk).start()
-    for block in range(blocks):
-        wave_copy(row_at(1), block).start()
-    inverse_copy.start()
-
+    for block in range(len(TRAILING)):
+        wave_copy(1, block).start()
     barrier = pltpu.get_barrier_semaphore()
     for direction in range(2):
         @pl.when(has_partner(direction))
@@ -128,23 +139,27 @@
             )
 
     lane = lax.broadcasted_iota(jnp.int32, (8, LANES), 1)
-    for chunk in range(CHUNKS):
-        bins = (2 * (lane + LANES * (chunk % 2)) + chunk // 2).astype(jnp.float32)
-        total_re = jnp.zeros_like(bins)
-        total_im = jnp.zeros_like(bins)
-        for process in range(2):
-            ratio = bins / freq_ref[process]
-            scaled = depth_ref[process] / (1.0 + ratio * ratio)
-            total_re = total_re + scaled * ratio * ratio
-            total_im = total_im + scaled * ratio
-        amplitude = jnp.exp(-total_re)
-        factors[0, chunk] = amplitude * jnp.cos(total_im)
-        factors[1, chunk] = -amplitude * jnp.sin(total_im)
-        factors[2, chunk] = (
-            RATE_TOP
-            * jnp.minimum(bins, 1.0)
-            * jnp.minimum(1.0, float(NT // 4) / jnp.maximum(bins, 1.0))
-        )
+    chunk_of = lax.broadcasted_iota(jnp.int32, (8, LANES), 0) & (CHUNKS - 1)
+    bins = (2 * (lane + LANES * (chunk_of & 1)) + (chunk_of >> 1)).astype(jnp.float32)
+    total_re = jnp.zeros_like(bins)
+    total_im = jnp.zeros_like(bins)
+    freq_copy.wait()
+    depth_copy.wait()
+    for process in range(2):
+        ratio = bins / freqs[process]
+        scaled = depths[process] / (1.0 + ratio * ratio)
+        total_re = total_re + scaled * ratio * ratio
+        total_im = total_im + scaled * ratio
+    amplitude = jnp.exp(-total_re)
+    rates = (
+        RATE_TOP
+        * jnp.minimum(bins, 1.0)
+        * jnp.minimum(1.0, float(NT // 4) / jnp.maximum(bins, 1.0))
+    )
+    table = (amplitude * jnp.cos(total_im), -amplitude * jnp.sin(total_im), rates)
+    for kind in range(3):
+        for chunk in range(CHUNKS):
+            factors[kind, chunk] = jnp.broadcast_to(table[kind][chunk:chunk + 1], (8, LANES))
 
     zero_rows = jnp.zeros((PAD, LANES), jnp.float32)
     for part in range(2):
@@ -158,32 +173,34 @@
     )
 
     def slot(message, direction):
-        return 2 * message + direction
+        return 2 * (message % SLOTS) + direction
 
     def send(message, part, chunk, direction, start=0, size=NY):
         return pltpu.make_async_remote_copy(
             src_ref=fields.at[part, chunk, direction, pl.ds(PAD + start, size)],
             dst_ref=landed.at[slot(message, direction), pl.ds(start, size)],
-            send_sem=send_sems.at[message, direction],
-            recv_sem=recv_sems.at[message, direction],
+            send_sem=send_sems.at[slot(message, direction)],
+            recv_sem=recv_sems.at[slot(message, direction)],
             device_id=device(partner(direction)),
             device_id_type=MESH,
         )
 
-    def forward_block(row, block, first):
-        rows = pl.ds(pl.multiple_of(block * BLOCK, BLOCK), BLOCK)
-        inner = pl.ds(pl.multiple_of(PAD + block * BLOCK, PAD), BLOCK)
-        wave_copy(row, block).wait()
+    def forward_block(turn, block):
+        row = row_at(turn)
+        sizes = (LEADING, TRAILING)[turn]
+        start, size = starts(sizes)[block], sizes[block]
+        rows, inner = pl.ds(start, size), pl.ds(PAD + start, size)
+        wave_copy(turn, block).wait()
         wave = waves[row, rows]
         squared = wave * wave
-        time = lax.broadcasted_iota(jnp.int32, (BLOCK, NT), 1)
+        time = lax.broadcasted_iota(jnp.int32, (size, NT), 1)
         after = jnp.where(time == NT - 1, 0.0, pltpu.roll(squared, NT - 1, 1))
         before = jnp.where(time == 0, 0.0, pltpu.roll(squared, 1, 1))
         steep = wave + WAVE_BREAKING * 0.25 * (after - before)
         early, late = steep[:, :HALF], steep[:, HALF:]
         pairs = (split_values(early + late), split_values(early - late))
         for chunk in range(CHUNKS):
-            if first:
+            if turn == 0 and block == 0:
                 table_copy(chunk).wait()
             high, low = pairs[chunk // 2]
             both = (
@@ -193,37 +210,30 @@
             factor_re = factors[0, chunk, 0:1]
             factor_im = factors[1, chunk, 0:1]
             fields[1, chunk, row, inner] = re * factor_im + im * factor_re
-            if chunk < EAGER:
+            if chunk < EAGER and turn == 0:
                 @pl.when(has_partner(row))
                 def _():
-                    send(chunk, 1, chunk, row, block * BLOCK, BLOCK).start()
+                    send(chunk, 1, chunk, row, start, size).start()
             fields[0, chunk, row, inner] = re * factor_re - im * factor_im
 
-    def forward_row(row, first):
-        if first:
-            forward_block(row, 0, True)
-
-        def one(block, carry):
-            forward_block(row, block, False)
-            return carry
-
-        lax.fori_loop(1 if first else 0, blocks, one, 0)
-
-        @pl.when(has_partner(row))
-        def _():
-            for chunk in range(EAGER, CHUNKS):
-                send(chunk, 1, chunk, row).start()
-
-    forward_row(row_at(0), True)
-    forward_row(row_at(1), False)
+    for turn in range(2):
+        for block in range(len((LEADING, TRAILING)[turn])):
+            forward_block(turn, block)
+
+        @pl.when(has_partner(row_at(turn)))
+        def _():
+            for chunk in range(EAGER if turn == 0 else 0, CHUNKS):
+                send(chunk, 1, chunk, row_at(turn)).start()
+
+    inverse_copy.start()
 
     @pl.when(jnp.logical_or(me == 0, me == count - 1))
     def _():
-        landed[2 * STEPS * CHUNKS] = jnp.zeros((NY, LANES), jnp.float32)
+        landed[2 * SLOTS] = jnp.zeros((NY, LANES), jnp.float32)
 
     def half_step(message, part, chunk, row, first_row=0, count_rows=NY):
         halo_from = 1 - row
-        at = jnp.where(has_partner(row), slot(message, halo_from), 2 * STEPS * CHUNKS)
+        at = jnp.where(has_partner(row), slot(message, halo_from), 2 * SLOTS)
         other = 1 - part
         sign = jnp.float32(2 * part - 1)
         rate = factors[2, chunk, 0:1] * sign
@@ -252,16 +262,22 @@
         high, low = split_values(fields[part, chunk, row, pl.ds(PAD + start, size)])
         return dot(jnp.concatenate([high, low, high], axis=1), inv[chunk, part])
 
-    def gather(part, chunk, fresh):
+    def gather(part, chunk, row, start, size, fresh=False, combined=False):
+        terms = terms_of(part, chunk, row, start, size)
+        rows = slice(start, start + size)
+        side = slice(0, HALF) if chunk < CHUNKS // 2 else slice(HALF, NT)
+        if fresh:
+            out_ref[row, rows, side] = terms
+        elif combined:
+            out_ref[row, rows, :HALF] += terms
+            out_ref[row, rows, HALF:] -= terms
+        else:
+            out_ref[row, rows, side] += terms
+
+    def gather_rows(part, chunk, **kind):
         for row in range(ROWS):
             for start in range(0, NY, GATHER):
-                terms = terms_of(part, chunk, row, start, GATHER)
-                rows = slice(start, start + GATHER)
-                side = slice(0, HALF) if chunk < CHUNKS // 2 else slice(HALF, NT)
-                if fresh:
-                    out_ref[row, rows, side] = terms
-                else:
-                    out_ref[row, rows, side] += terms
+                gather(part, chunk, row, start, GATHER, **kind)
 
     def advance(message, carry):
         step = message // CHUNKS
@@ -287,11 +303,10 @@
     lax.fori_loop(0, (STEPS - 2) * CHUNKS, advance, 0)
     inverse_copy.wait()
 
-    piece_rows = NY // PIECES
     last = STEPS * CHUNKS - 1
 
     def piece_copy(piece, direction):
-        start = piece * piece_rows
+        start, piece_rows = starts(PIECES)[piece], PIECES[piece]
         return pltpu.make_async_remote_copy(
             src_ref=fields.at[0, CHUNKS - 1, direction, pl.ds(PAD + start, piece_rows)],
             dst_ref=landed.at[slot(last, direction), pl.ds(start, piece_rows)],
@@ -315,8 +330,8 @@
             def _():
                 send(message + CHUNKS, 0, chunk, leaving).start()
         else:
-            for piece in range(PIECES):
-                half_step(message, 0, chunk, leaving, piece * piece_rows, piece_rows)
+            for piece in range(len(PIECES)):
+                half_step(message, 0, chunk, leaving, starts(PIECES)[piece], PIECES[piece])
 
                 @pl.when(has_partner(leaving))
                 def _():
@@ -328,7 +343,12 @@
         def _():
             send(message + CHUNKS, 0, chunk, staying).start()
 
-        gather(0, chunk, chunk % 2 == 0)
+        gather_rows(0, chunk, fresh=chunk % 2 == 0)
+
+    def combine(row, rows):
+        even, odd = out_ref[row, rows, :HALF], out_ref[row, rows, HALF:]
+        out_ref[row, rows, :HALF] = even + odd
+        out_ref[row, rows, HALF:] = even - odd
 
     for chunk in range(CHUNKS - 1):
         message = (STEPS - 1) * CHUNKS + chunk
@@ -337,72 +357,64 @@
         for row in (staying, leaving):
             wait_for(message, 1, chunk, row)
             half_step(message, 1, chunk, row)
-        gather(1, chunk, False)
-
-    def combine(row, rows):
-        even, odd = out_ref[row, rows, :HALF], out_ref[row, rows, HALF:]
-        out_ref[row, rows, :HALF] = even + odd
-        out_ref[row, rows, HALF:] = even - odd
-
-    for row in range(ROWS):
-        for start in range(0, NY, 64):
-            combine(row, slice(start, start + 64))
+        gather_rows(1, chunk, combined=chunk >= CHUNKS // 2)
+        if chunk == CHUNKS // 2 - 1:
+            for row in range(ROWS):
+                for start in range(0, NY, 64):
+                    combine(row, slice(start, start + 64))
 
     def finish(row, start, size):
         half_step(last, 1, CHUNKS - 1, row, start, size)
-        terms = terms_of(1, CHUNKS - 1, row, start, size)
-        rows = slice(start, start + size)
-        out_ref[row, rows, :HALF] += terms
-        out_ref[row, rows, HALF:] -= terms
+        gather(1, CHUNKS - 1, row, start, size, combined=True)
 
     for direction in range(2):
         wait_sent(last - CHUNKS, 0, CHUNKS - 1, direction)
     wait_for(last, 1, CHUNKS - 1, staying)
     for start in range(0, NY, GATHER):
         finish(staying, start, GATHER)
-    for piece in range(PIECES):
+    for piece in range(len(PIECES)):
         @pl.when(has_partner(leaving))
         def _():
             piece_copy(piece, 1 - leaving).wait_recv()
 
-        finish(leaving, piece * piece_rows, piece_rows)
+        finish(leaving, starts(PIECES)[piece], PIECES[piece])
 
     for chunk in range(CHUNKS):
         message = (STEPS - 1) * CHUNKS + chunk
         wait_sent(message, 1, chunk, staying)
         if chunk < CHUNKS - 1:
             wait_sent(message, 1, chunk, leaving)
-    for piece in range(PIECES):
+    for piece in range(len(PIECES)):
         @pl.when(has_partner(leaving))
         def _():
             piece_copy(piece, leaving).wait_send()
 
 
 def shards(narrow_size, wide_size, pressure, relax_freq, relax_depth):
-    blocks = NY // BLOCK
-    messages = STEPS * CHUNKS
     hbm = pl.BlockSpec(memory_space=pltpu.HBM)
-    smem = pl.BlockSpec(memory_space=pltpu.SMEM)
     f32, bf16 = jnp.float32, jnp.bfloat16
     dma = pltpu.SemaphoreType.DMA
     return pl.pallas_call(
         functools.partial(step_kernel, narrow_size, wide_size),
         out_shape=pltpu.VMEM((ROWS, NY, NT), f32),
-        in_specs=[smem, smem, hbm, hbm, hbm],
+        in_specs=[hbm, hbm, hbm, hbm, hbm],
         out_specs=pl.BlockSpec(memory_space=pltpu.VMEM),
         scratch_shapes=[
             pltpu.VMEM((ROWS, NY, NT), f32),
             pltpu.VMEM((2, CHUNKS, ROWS, NY + 2 * PAD, LANES), f32),
-            pltpu.VMEM((2 * messages + 1, NY, LANES), f32),
+            pltpu.VMEM((2 * SLOTS + 1, NY, LANES), f32),
             pltpu.VMEM((CHUNKS, 2, HALF, 2 * LANES), bf16),
             pltpu.VMEM((CHUNKS, 2, 3 * LANES, HALF), bf16),
             pltpu.VMEM((3, CHUNKS, 8, LANES), f32),
-            dma((ROWS, blocks)),
+            pltpu.SMEM((2,), f32),
+            pltpu.SMEM((2,), f32),
+            dma((len(LEADING) + len(TRAILING),)),
             dma((CHUNKS + 1,)),
-            dma((messages, 2)),
-            dma((messages, 2)),
-            dma((PIECES,)),
-            dma((PIECES,)),
+            dma((2,)),
+            dma((2 * SLOTS,)),
+            dma((2 * SLOTS,)),
+            dma((len(PIECES),)),
+            dma((len(PIECES),)),
         ],
         compiler_params=pltpu.CompilerParams(
             collective_id=0, has_side_effects=True, vmem_limit_bytes=59 * 2**20

time: 82.2 us -> 80.6 us (0.981)
  Pallas kernels: 80.1 us -> 78.6 us
    pallas_call x1, Pallas kernels: 80.1 us -> 78.6 us  [shards(): pl.pallas_call(functools.partial(step_kernel, narrow_size, wide_size), ou...]
where the time goes in v2:
time: 80.6 us
  Pallas kernels  78.6 us (98%)
  local copies, waits for them, and re-layouts  2.02 us (3%)
    pallas_call x1, Pallas kernels, shards(): pl.pallas_call(functools.partial(step_kernel, narrow_size, wide_size), ou...  78.6 us
    unnamed x1, local copies, waits for them, and re-layouts  2.02 us

profile of v2, /device:TPU:6, one launch (start us, length us, event | category | flops | bytes accessed | tf_op | source)
XLA Modules:
  0.0 80.6 jit_solution(1351546673439367686)
XLA Ops:
  0.0 78.6 %shard_map.55 = f32[2,512,1024]{2,1,0:T(8,128)S(1)} custom-call(f32[2]{0:T(128)} %freq_ref.1, f32[2]{0:T(128)} %depth_ref.1, f32[2,512,1024]{2,1,0:T(8,128)} %pressure_ref.1, bf16[4,2,512,256]{3,2,1,0:T(8,128)(2,1)} %constant.4.clone.forward_ref, bf16[4,2,384,512]{3,2,1,0:T(8,128)(2,1)} %constant.5.clone.inverse_ref), custom_call_target="tpu_custom_call" | custom-call | flops 6442450944 | bytes 14680064 | tf_op jit(solution)/shard_map/pallas_call | solution.py:397
  78.6 2.0 %copy.7 = f32[2,512,1024]{2,1,0:T(8,128)} copy(f32[2,512,1024]{2,1,0:T(8,128)S(1)} %shard_map.55) | data formatting | bytes 8388608

commit v3 on v2

--- a/solution.py
+++ b/solution.py
@@ -1,4 +1,5 @@
 import functools
+import math
 
 import jax
 import jax.numpy as jnp
@@ -28,6 +29,7 @@
 SLOTS = 2 * CHUNKS
 ROWS = 2
 MESH = pl.DeviceIdType.MESH
+ROOT_HALF = math.sqrt(0.5)
 
 
 def starts(sizes):
@@ -35,7 +37,29 @@
 
 
 def chunk_bins(chunk):
-    return 2 * (np.arange(LANES) + LANES * (chunk % 2)) + chunk // 2
+    lane = np.arange(LANES)
+    if chunk < 2:
+        return 4 * lane + 2 * chunk, np.ones(LANES)
+    bins = 8 * lane + 1 + 4 * (chunk - 2)
+    mirrored = bins > HALF
+    return np.where(mirrored, NT - bins, bins), np.where(mirrored, -1.0, 1.0)
+
+
+def chunk_table(chunk):
+    bins, sign = chunk_bins(chunk)
+    at = np.where(sign < 0, NT - bins, bins)
+    time = np.arange(2 * LANES if chunk < 2 else LANES)
+    angle = 2.0 * np.pi * (time[:, None] * at[None, :] % NT) / NT
+    cosine, sine = np.cos(angle), np.sin(angle)
+    if chunk < 2:
+        return np.concatenate([cosine, -sine], axis=1)
+    return np.concatenate(
+        [
+            np.concatenate([cosine, -sine * sign], axis=1),
+            np.concatenate([-sine, -cosine * sign], axis=1),
+        ],
+        axis=0,
+    )
 
 
 def split_table(table):
@@ -45,27 +69,41 @@
 
 
 def forward_tables():
-    time = np.arange(HALF)
+    return np.stack([np.stack(split_table(chunk_table(chunk))) for chunk in range(CHUNKS)])
+
+
+def inverse_tables():
     tables = []
     for chunk in range(CHUNKS):
-        angle = 2.0 * np.pi * (time[:, None] * chunk_bins(chunk)[None, :] % NT) / NT
-        tables.append(split_table(np.concatenate([np.cos(angle), -np.sin(angle)], axis=1)))
-    return np.stack([np.stack(pair) for pair in tables])
-
-
-def inverse_tables():
-    time = np.arange(HALF)
-    tables = []
-    for chunk in range(CHUNKS):
-        bins = chunk_bins(chunk)
-        angle = 2.0 * np.pi * (bins[:, None] * time[None, :] % NT) / NT
-        weight = (np.where(bins == 0, 1.0, 2.0) / NT)[:, None]
+        weight = (np.where(chunk_bins(chunk)[0] == 0, 1.0, 2.0) / NT)[:, None]
         parts = []
-        for table in (np.cos(angle) * weight, -np.sin(angle) * weight):
-            high, low = split_table(table)
+        for part in range(2):
+            columns = slice(part * LANES, (part + 1) * LANES)
+            high, low = split_table(chunk_table(chunk)[:, columns].T * weight)
             parts.append(np.concatenate([high, high, low], axis=0))
         tables.append(np.stack(parts))
     return np.stack(tables)
+
+
+def fold(groups):
+    u = [groups[index] + groups[index + 4] for index in range(4)]
+    v = [groups[index] - groups[index + 4] for index in range(4)]
+    across = (v[1] - v[3]) * ROOT_HALF
+    along = (v[1] + v[3]) * ROOT_HALF
+    return (
+        (u[0] + u[2], u[1] + u[3]),
+        (u[0] - u[2], u[1] - u[3]),
+        (v[0] + across, v[2] + along),
+        (v[0] - across, v[2] - along),
+    )
+
+
+def unfold(sums):
+    (a0, a1), (b0, b1), (p0, p1), (q0, q1) = sums
+    u = (a0 + b0, a1 + b1, a0 - b0, a1 - b1)
+    across, along = p0 - q0, p1 - q1
+    v = (p0 + q0, (along + across) * ROOT_HALF, p1 + q1, (along - across) * ROOT_HALF)
+    return [u[index] + v[index] for index in range(4)] + [u[index] - v[index] for index in range(4)]
 
 
 def split_values(values):
@@ -140,7 +178,9 @@
 
     lane = lax.broadcasted_iota(jnp.int32, (8, LANES), 1)
     chunk_of = lax.broadcasted_iota(jnp.int32, (8, LANES), 0) & (CHUNKS - 1)
-    bins = (2 * (lane + LANES * (chunk_of & 1)) + (chunk_of >> 1)).astype(jnp.float32)
+    counted = 8 * lane + 4 * chunk_of - 7
+    odd = jnp.where(counted > HALF, NT - counted, counted)
+    bins = jnp.where(chunk_of < 2, 4 * lane + 2 * chunk_of, odd).astype(jnp.float32)
     total_re = jnp.zeros_like(bins)
     total_im = jnp.zeros_like(bins)
     freq_copy.wait()
@@ -197,12 +237,11 @@
         after = jnp.where(time == NT - 1, 0.0, pltpu.roll(squared, NT - 1, 1))
         before = jnp.where(time == 0, 0.0, pltpu.roll(squared, 1, 1))
         steep = wave + WAVE_BREAKING * 0.25 * (after - before)
-        early, late = steep[:, :HALF], steep[:, HALF:]
-        pairs = (split_values(early + late), split_values(early - late))
+        folded = fold([steep[:, at:at + LANES] for at in range(0, NT, LANES)])
         for chunk in range(CHUNKS):
             if turn == 0 and block == 0:
                 table_copy(chunk).wait()
-            high, low = pairs[chunk // 2]
+            high, low = split_values(jnp.concatenate(folded[chunk], axis=1))
             both = (
                 dot(high, fwd[chunk, 0]) + dot(low, fwd[chunk, 0]) + dot(high, fwd[chunk, 1])
             )
@@ -262,22 +301,18 @@
         high, low = split_values(fields[part, chunk, row, pl.ds(PAD + start, size)])
         return dot(jnp.concatenate([high, low, high], axis=1), inv[chunk, part])
 
-    def gather(part, chunk, row, start, size, fresh=False, combined=False):
-        terms = terms_of(part, chunk, row, start, size)
-        rows = slice(start, start + size)
-        side = slice(0, HALF) if chunk < CHUNKS // 2 else slice(HALF, NT)
-        if fresh:
-            out_ref[row, rows, side] = terms
-        elif combined:
-            out_ref[row, rows, :HALF] += terms
-            out_ref[row, rows, HALF:] -= terms
-        else:
-            out_ref[row, rows, side] += terms
-
-    def gather_rows(part, chunk, **kind):
+    def sums_of(chunk):
+        return slice(2 * LANES * chunk, 2 * LANES * (chunk + 1))
+
+    def gather_rows(part, chunk):
         for row in range(ROWS):
             for start in range(0, NY, GATHER):
-                gather(part, chunk, row, start, GATHER, **kind)
+                terms = terms_of(part, chunk, row, start, GATHER)
+                rows = slice(start, start + GATHER)
+                if part == 0:
+                    out_ref[row, rows, sums_of(chunk)] = terms
+                else:
+                    out_ref[row, rows, sums_of(chunk)] += terms
 
     def advance(message, carry):
         step = message // CHUNKS
@@ -343,12 +378,7 @@
         def _():
             send(message + CHUNKS, 0, chunk, staying).start()
 
-        gather_rows(0, chunk, fresh=chunk % 2 == 0)
-
-    def combine(row, rows):
-        even, odd = out_ref[row, rows, :HALF], out_ref[row, rows, HALF:]
-        out_ref[row, rows, :HALF] = even + odd
-        out_ref[row, rows, HALF:] = even - odd
+        gather_rows(0, chunk)
 
     for chunk in range(CHUNKS - 1):
         message = (STEPS - 1) * CHUNKS + chunk
@@ -357,15 +387,20 @@
         for row in (staying, leaving):
             wait_for(message, 1, chunk, row)
             half_step(message, 1, chunk, row)
-        gather_rows(1, chunk, combined=chunk >= CHUNKS // 2)
-        if chunk == CHUNKS // 2 - 1:
-            for row in range(ROWS):
-                for start in range(0, NY, 64):
-                    combine(row, slice(start, start + 64))
+        gather_rows(1, chunk)
 
     def finish(row, start, size):
         half_step(last, 1, CHUNKS - 1, row, start, size)
-        gather(1, CHUNKS - 1, row, start, size, combined=True)
+        terms = terms_of(1, CHUNKS - 1, row, start, size)
+        rows = slice(start, start + size)
+        out_ref[row, rows, sums_of(CHUNKS - 1)] += terms
+        step = 64
+        for at in range(start, start + size, step):
+            rows = slice(at, at + step)
+            groups = [out_ref[row, rows, lane:lane + LANES] for lane in range(0, NT, LANES)]
+            whole = unfold([(groups[2 * chunk], groups[2 * chunk + 1]) for chunk in range(CHUNKS)])
+            for index in range(2 * CHUNKS):
+                out_ref[row, rows, index * LANES:(index + 1) * LANES] = whole[index]
 
     for direction in range(2):
         wait_sent(last - CHUNKS, 0, CHUNKS - 1, direction)
@@ -403,8 +438,8 @@
             pltpu.VMEM((ROWS, NY, NT), f32),
             pltpu.VMEM((2, CHUNKS, ROWS, NY + 2 * PAD, LANES), f32),
             pltpu.VMEM((2 * SLOTS + 1, NY, LANES), f32),
-            pltpu.VMEM((CHUNKS, 2, HALF, 2 * LANES), bf16),
-            pltpu.VMEM((CHUNKS, 2, 3 * LANES, HALF), bf16),
+            pltpu.VMEM((CHUNKS, 2, 2 * LANES, 2 * LANES), bf16),
+            pltpu.VMEM((CHUNKS, 2, 3 * LANES, 2 * LANES), bf16),
             pltpu.VMEM((3, CHUNKS, 8, LANES), f32),
             pltpu.SMEM((2,), f32),
             pltpu.SMEM((2,), f32),
@@ -420,7 +455,7 @@
             collective_id=0, has_side_effects=True, vmem_limit_bytes=59 * 2**20
         ),
         cost_estimate=pl.CostEstimate(
-            flops=2 * 2 * 3 * ROWS * NY * HALF * NT, bytes_accessed=14 * 2**20, transcendentals=0
+            flops=2 * 2 * 3 * ROWS * NY * 2 * LANES * NT, bytes_accessed=14 * 2**20, transcendentals=0
         ),
     )(relax_freq, relax_depth, pressure, jnp.asarray(forward_tables()), jnp.asarray(inverse_tables()))
 

time: 80.6 us -> 79.9 us (level)
  no operation moved by 1% of the time
where the time goes in v3:
time: 79.9 us; the launch traced here: 79.8 us
  Pallas kernels  77.8 us (97%)
  local copies, waits for them, and re-layouts  2.02 us (3%)
    pallas_call x1, Pallas kernels, shards(): pl.pallas_call(functools.partial(step_kernel, narrow_size, wide_size), ou...  77.8 us
    unnamed x1, local copies, waits for them, and re-layouts  2.02 us

profile of v3, /device:TPU:6, one launch (start us, length us, event | category | flops | bytes accessed | tf_op | source)
XLA Modules:
  0.0 79.8 jit_solution(3979147697484279063)
XLA Ops:
  0.0 77.8 %shard_map.55 = f32[2,512,1024]{2,1,0:T(8,128)S(1)} custom-call(f32[2]{0:T(128)} %freq_ref.1, f32[2]{0:T(128)} %depth_ref.1, f32[2,512,1024]{2,1,0:T(8,128)} %pressure_ref.1, bf16[4,2,256,256]{3,2,1,0:T(8,128)(2,1)} %constant.4.clone.forward_ref, bf16[4,2,384,256]{3,2,1,0:T(8,128)(2,1)} %constant.5.clone.inverse_ref), custom_call_target="tpu_custom_call" | custom-call | flops 3221225472 | bytes 14680064 | tf_op jit(solution)/shard_map/pallas_call | solution.py:432
  77.8 2.0 %copy.7 = f32[2,512,1024]{2,1,0:T(8,128)} copy(f32[2,512,1024]{2,1,0:T(8,128)S(1)} %shard_map.55) | data formatting | bytes 8388608

commit v4 on v3

--- a/solution.py
+++ b/solution.py
@@ -22,8 +22,8 @@
 CHUNKS = (NT // 2) // LANES
 PAD = 8
 LEADING = (96, 416)
-TRAILING = (256, 256)
-GATHER = 256
+TRAILING = (512,)
+GATHER = 512
 PIECES = (384, 128)
 EAGER = 4
 SLOTS = 2 * CHUNKS
@@ -140,6 +140,14 @@
     def row_at(turn):
         return lax.rem(core + turn, 2)
 
+    barrier = pltpu.get_barrier_semaphore()
+    for direction in range(2):
+        @pl.when(has_partner(direction))
+        def _():
+            pl.semaphore_signal(
+                barrier, inc=1, device_id=device(partner(direction)), device_id_type=MESH
+            )
+
     def wave_copy(turn, block):
         sizes = (LEADING, TRAILING)[turn]
         rows = pl.ds(starts(sizes)[block], sizes[block])
@@ -168,14 +176,32 @@
         table_copy(chunk).start()
     for block in range(len(TRAILING)):
         wave_copy(1, block).start()
-    barrier = pltpu.get_barrier_semaphore()
-    for direction in range(2):
-        @pl.when(has_partner(direction))
-        def _():
-            pl.semaphore_signal(
-                barrier, inc=1, device_id=device(partner(direction)), device_id_type=MESH
-            )
-
+    zero_rows = jnp.zeros((PAD, LANES), jnp.float32)
+    for part in range(2):
+        for chunk in range(CHUNKS):
+            for row in range(ROWS):
+                fields[part, chunk, row, 0:PAD] = zero_rows
+                fields[part, chunk, row, PAD + NY:] = zero_rows
+
+    pl.semaphore_wait(
+        barrier, has_partner(0).astype(jnp.int32) + has_partner(1).astype(jnp.int32)
+    )
+
+    def slot(message, direction):
+        return 2 * (message % SLOTS) + direction
+
+    def send(message, part, chunk, direction, start=0, size=NY):
+        return pltpu.make_async_remote_copy(
+            src_ref=fields.at[part, chunk, direction, pl.ds(PAD + start, size)],
+            dst_ref=landed.at[slot(message, direction), pl.ds(start, size)],
+            send_sem=send_sems.at[slot(message, direction)],
+            recv_sem=recv_sems.at[slot(message, direction)],
+            device_id=device(partner(direction)),
+            device_id_type=MESH,
+        )
+
+    wave_copy(0, 0).wait()
+    table_copy(0).wait()
     lane = lax.broadcasted_iota(jnp.int32, (8, LANES), 1)
     chunk_of = lax.broadcasted_iota(jnp.int32, (8, LANES), 0) & (CHUNKS - 1)
     counted = 8 * lane + 4 * chunk_of - 7
@@ -201,36 +227,13 @@
         for chunk in range(CHUNKS):
             factors[kind, chunk] = jnp.broadcast_to(table[kind][chunk:chunk + 1], (8, LANES))
 
-    zero_rows = jnp.zeros((PAD, LANES), jnp.float32)
-    for part in range(2):
-        for chunk in range(CHUNKS):
-            for row in range(ROWS):
-                fields[part, chunk, row, 0:PAD] = zero_rows
-                fields[part, chunk, row, PAD + NY:] = zero_rows
-
-    pl.semaphore_wait(
-        barrier, has_partner(0).astype(jnp.int32) + has_partner(1).astype(jnp.int32)
-    )
-
-    def slot(message, direction):
-        return 2 * (message % SLOTS) + direction
-
-    def send(message, part, chunk, direction, start=0, size=NY):
-        return pltpu.make_async_remote_copy(
-            src_ref=fields.at[part, chunk, direction, pl.ds(PAD + start, size)],
-            dst_ref=landed.at[slot(message, direction), pl.ds(start, size)],
-            send_sem=send_sems.at[slot(message, direction)],
-            recv_sem=recv_sems.at[slot(message, direction)],
-            device_id=device(partner(direction)),
-            device_id_type=MESH,
-        )
-
     def forward_block(turn, block):
         row = row_at(turn)
         sizes = (LEADING, TRAILING)[turn]
         start, size = starts(sizes)[block], sizes[block]
         rows, inner = pl.ds(start, size), pl.ds(PAD + start, size)
-        wave_copy(turn, block).wait()
+        if turn + block > 0:
+            wave_copy(turn, block).wait()
         wave = waves[row, rows]
         squared = wave * wave
         time = lax.broadcasted_iota(jnp.int32, (size, NT), 1)
@@ -239,7 +242,7 @@
         steep = wave + WAVE_BREAKING * 0.25 * (after - before)
         folded = fold([steep[:, at:at + LANES] for at in range(0, NT, LANES)])
         for chunk in range(CHUNKS):
-            if turn == 0 and block == 0:
+            if turn + block == 0 and chunk > 0:
                 table_copy(chunk).wait()
             high, low = split_values(jnp.concatenate(folded[chunk], axis=1))
             both = (

time: 79.9 us -> 79.8 us (level)
  no operation moved by 1% of the time
where the time goes in v4:
time: 79.8 us; the launch traced here: 79.7 us
  Pallas kernels  77.7 us (97%)
  local copies, waits for them, and re-layouts  2.02 us (3%)
    pallas_call x1, Pallas kernels, shards(): pl.pallas_call(functools.partial(step_kernel, narrow_size, wide_size), ou...  77.7 us
    unnamed x1, local copies, waits for them, and re-layouts  2.02 us

profile of v4, /device:TPU:6, one launch (start us, length us, event | category | flops | bytes accessed | tf_op | source)
XLA Modules:
  0.0 79.7 jit_solution(10276749803968714637)
XLA Ops:
  0.0 77.7 %shard_map.55 = f32[2,512,1024]{2,1,0:T(8,128)S(1)} custom-call(f32[2]{0:T(128)} %freq_ref.1, f32[2]{0:T(128)} %depth_ref.1, f32[2,512,1024]{2,1,0:T(8,128)} %pressure_ref.1, bf16[4,2,256,256]{3,2,1,0:T(8,128)(2,1)} %constant.4.clone.forward_ref, bf16[4,2,384,256]{3,2,1,0:T(8,128)(2,1)} %constant.5.clone.inverse_ref), custom_call_target="tpu_custom_call" | custom-call | flops 3221225472 | bytes 14680064 | tf_op jit(solution)/shard_map/pallas_call | solution.py:435
  77.7 2.0 %copy.7 = f32[2,512,1024]{2,1,0:T(8,128)} copy(f32[2,512,1024]{2,1,0:T(8,128)S(1)} %shard_map.55) | data formatting | bytes 8388608

commit v5 on v4

--- a/solution.py
+++ b/solution.py
@@ -183,9 +183,6 @@
                 fields[part, chunk, row, 0:PAD] = zero_rows
                 fields[part, chunk, row, PAD + NY:] = zero_rows
 
-    pl.semaphore_wait(
-        barrier, has_partner(0).astype(jnp.int32) + has_partner(1).astype(jnp.int32)
-    )
 
     def slot(message, direction):
         return 2 * (message % SLOTS) + direction
@@ -252,6 +249,9 @@
             factor_re = factors[0, chunk, 0:1]
             factor_im = factors[1, chunk, 0:1]
             fields[1, chunk, row, inner] = re * factor_im + im * factor_re
+            if turn + block + chunk == 0:
+                peers = has_partner(0).astype(jnp.int32) + has_partner(1).astype(jnp.int32)
+                pl.semaphore_wait(barrier, peers)
             if chunk < EAGER and turn == 0:
                 @pl.when(has_partner(row))
                 def _():

time: 79.8 us -> 79.8 us (level)
  no operation moved by 1% of the time
where the time goes in v5:
time: 79.8 us; the launch traced here: 79.7 us
  Pallas kernels  77.7 us (97%)
  local copies, waits for them, and re-layouts  2.02 us (3%)
    pallas_call x1, Pallas kernels, shards(): pl.pallas_call(functools.partial(step_kernel, narrow_size, wide_size), ou...  77.7 us
    unnamed x1, local copies, waits for them, and re-layouts  2.02 us

profile of v5, /device:TPU:6, one launch (start us, length us, event | category | flops | bytes accessed | tf_op | source)
XLA Modules:
  0.0 79.7 jit_solution(183062339626559400)
XLA Ops:
  0.0 77.7 %shard_map.55 = f32[2,512,1024]{2,1,0:T(8,128)S(1)} custom-call(f32[2]{0:T(128)} %freq_ref.1, f32[2]{0:T(128)} %depth_ref.1, f32[2,512,1024]{2,1,0:T(8,128)} %pressure_ref.1, bf16[4,2,256,256]{3,2,1,0:T(8,128)(2,1)} %constant.4.clone.forward_ref, bf16[4,2,384,256]{3,2,1,0:T(8,128)(2,1)} %constant.5.clone.inverse_ref), custom_call_target="tpu_custom_call" | custom-call | flops 3221225472 | bytes 14680064 | tf_op jit(solution)/shard_map/pallas_call | solution.py:435
  77.7 2.0 %copy.7 = f32[2,512,1024]{2,1,0:T(8,128)} copy(f32[2,512,1024]{2,1,0:T(8,128)S(1)} %shard_map.55) | data formatting | bytes 8388608

commit v6 on v4

--- a/solution.py
+++ b/solution.py
@@ -158,9 +158,12 @@
         )
 
     def table_copy(chunk):
-        return pltpu.make_async_copy(forward_ref.at[chunk], fwd.at[chunk], table_sems.at[chunk])
-
-    inverse_copy = pltpu.make_async_copy(inverse_ref, inv, table_sems.at[CHUNKS])
+        chunks = pl.ds(0, 1) if chunk == 0 else pl.ds(1, CHUNKS - 1)
+        return pltpu.make_async_copy(
+            forward_ref.at[chunks], fwd.at[chunks], table_sems.at[min(chunk, 1)]
+        )
+
+    inverse_copy = pltpu.make_async_copy(inverse_ref, inv, table_sems.at[2])
     freq_copy = pltpu.make_async_copy(freq_ref, freqs, scalar_sems.at[0])
     depth_copy = pltpu.make_async_copy(depth_ref, depths, scalar_sems.at[1])
 
@@ -172,8 +175,6 @@
     table_copy(1).start()
     for block in range(2, len(LEADING)):
         wave_copy(0, block).start()
-    for chunk in range(2, CHUNKS):
-        table_copy(chunk).start()
     for block in range(len(TRAILING)):
         wave_copy(1, block).start()
     zero_rows = jnp.zeros((PAD, LANES), jnp.float32)
@@ -242,7 +243,7 @@
         steep = wave + WAVE_BREAKING * 0.25 * (after - before)
         folded = fold([steep[:, at:at + LANES] for at in range(0, NT, LANES)])
         for chunk in range(CHUNKS):
-            if turn + block == 0 and chunk > 0:
+            if turn + block == 0 and chunk == 1:
                 table_copy(chunk).wait()
             high, low = split_values(jnp.concatenate(folded[chunk], axis=1))
             both = (
@@ -447,7 +448,7 @@
             pltpu.SMEM((2,), f32),
             pltpu.SMEM((2,), f32),
             dma((len(LEADING) + len(TRAILING),)),
-            dma((CHUNKS + 1,)),
+            dma((3,)),
             dma((2,)),
             dma((2 * SLOTS,)),
             dma((2 * SLOTS,)),

time: 79.8 us -> 80 us (level)
  no operation moved by 1% of the time
where the time goes in v6:
time: 80 us; the launch traced here: 79.9 us
  Pallas kernels  77.9 us (97%)
  local copies, waits for them, and re-layouts  2.02 us (3%)
    pallas_call x1, Pallas kernels, shards(): pl.pallas_call(functools.partial(step_kernel, narrow_size, wide_size), ou...  77.9 us
    unnamed x1, local copies, waits for them, and re-layouts  2.02 us

profile of v6, /device:TPU:6, one launch (start us, length us, event | category | flops | bytes accessed | tf_op | source)
XLA Modules:
  0.0 79.9 jit_solution(16786893069494538271)
XLA Ops:
  0.0 77.9 %shard_map.55 = f32[2,512,1024]{2,1,0:T(8,128)S(1)} custom-call(f32[2]{0:T(128)} %freq_ref.1, f32[2]{0:T(128)} %depth_ref.1, f32[2,512,1024]{2,1,0:T(8,128)} %pressure_ref.1, bf16[4,2,256,256]{3,2,1,0:T(8,128)(2,1)} %constant.4.clone.forward_ref, bf16[4,2,384,256]{3,2,1,0:T(8,128)(2,1)} %constant.5.clone.inverse_ref), custom_call_target="tpu_custom_call" | custom-call | flops 3221225472 | bytes 14680064 | tf_op jit(solution)/shard_map/pallas_call | solution.py:436
  77.9 2.0 %copy.7 = f32[2,512,1024]{2,1,0:T(8,128)} copy(f32[2,512,1024]{2,1,0:T(8,128)S(1)} %shard_map.55) | data formatting | bytes 8388608
